TPU v7x, 256 devices: a whole 4x4x8 slice. The times are simulated.
256 devices in a mesh: row: 8 (over y, core), col: 32 (over x, z).
Axes of the slice: x: 4, y: 4, z: 8, core: 2. Of those that a mesh axis runs over, the one named last changes fastest.
Arguments:
- span: bfloat16 [1024, 16384], P('col', 'row'), may hold values from -6 to 6
- gram: float32 [16384, 16384], P('row', 'col'), may hold values from -0.08 to 0.08
- ridge: float32 [16384], P('row'), may hold values from 4 to 8
Outputs:
- factored: float32 [16384, 16384], P('row', 'col')
All inputs are finite; a program needn't handle non-finite values.
Results may differ from a plain program's by a relative error of at most 0.005.
Values may be sent and summed in bfloat16 or wider, within the bound.
A program may use at most 64 MiB of HBM per device.

v0:
```python
import jax
import jax.numpy as jnp
from jax import lax
from jax.sharding import PartitionSpec as P

NB = 512


def from_root(block, axis, source):
    block = jnp.where(lax.axis_index(axis) == source, block, jnp.zeros_like(block))
    return lax.psum(block, axis)


def as_sent(x):
    return jax.tree.map(lambda a: a.astype(jnp.bfloat16) if a.dtype == jnp.float32 else a, x)


def factor_corner(corner):
    symmetric = jnp.tril(corner) + jnp.tril(corner, -1).T
    return jnp.linalg.cholesky(symmetric)


def apply_factor(lower_part, panel_source):
    return jax.scipy.linalg.solve_triangular(lower_part, panel_source.T, lower=True).T


def finish_panel(lower_part, panel_source, head_rows):
    solved = apply_factor(lower_part, panel_source)
    rows_local = panel_source.shape[0]
    width = lower_part.shape[0]
    padded = jnp.concatenate(
        [lower_part, jnp.zeros((rows_local - width, width), jnp.float32)], axis=0
    )
    return jnp.where(head_rows, padded, solved)


def on_device(span, gram, ridge):
    row_count = lax.axis_size("row")
    col_count = lax.axis_size("col")
    row_place = lax.axis_index("row")
    col_place = lax.axis_index("col")
    rows_local, cols_local = gram.shape
    width = NB
    col_tiles = cols_local // width
    tok_local = span.shape[0]
    token_total = tok_local * col_count
    full = lax.all_gather(span, "row", axis=1, tiled=True)
    total_width = full.shape[1]
    within_rows = total_width // (row_count * width)
    logical = (
        full.reshape(tok_local, row_count, within_rows, width)
        .transpose(0, 2, 1, 3)
        .reshape(tok_local, total_width)
    )
    grouped = logical.reshape(tok_local, col_tiles, col_count, width).transpose(0, 2, 1, 3)
    grouped = grouped.reshape(tok_local, col_count, cols_local)
    moved = lax.all_to_all(grouped, "col", split_axis=1, concat_axis=0, tiled=True)
    span_cols = moved.reshape(token_total, cols_local)
    product = lax.dot_general(
        lax.all_gather(span, "col", axis=0, tiled=True),
        span_cols,
        (((0,), (0,)), ((), ())),
        preferred_element_type=jnp.float32,
    )
    row_pos = jnp.arange(rows_local, dtype=jnp.int32)
    col_pos = jnp.arange(cols_local, dtype=jnp.int32)
    row_logical = (row_pos // width * row_count + row_place) * width + row_pos % width
    col_logical = (col_pos // width * col_count + col_place) * width + col_pos % width
    on_diagonal = row_logical[:, None] == col_logical[None, :]
    accum = gram + product / token_total + jnp.where(on_diagonal, ridge[:, None], 0.0)
    head_rows = row_logical[:, None] < width
    corner = from_root(accum[:width, :width].astype(jnp.bfloat16), "row", 0).astype(jnp.float32)
    lower_part = factor_corner(corner)
    panel = from_root(finish_panel(lower_part, accum, head_rows), "col", 0)
    tile_number = 0 + col_place
    part_rows = lax.dynamic_slice_in_dim(panel, tile_number // row_count * width, width, 0)
    matched_parts = from_root(as_sent(part_rows), "row", tile_number % row_count).astype(
        part_rows.dtype
    )
    update = lax.dot_general(
        panel,
        matched_parts,
        (((1,), (1,)), ((), ())),
        precision=lax.Precision.HIGHEST,
        preferred_element_type=jnp.float32,
    )
    trailing = jnp.where(head_rows, accum, accum - update)
    panel_full = jnp.concatenate(
        [panel, jnp.zeros((rows_local, cols_local - width), jnp.float32)], axis=1
    )
    return jnp.where(col_logical[None, :] < width, panel_full, trailing)


def solution(mesh):
    placed = (P("col", "row"), P("row", "col"), P("row"))
    return jax.shard_map(
        on_device, mesh=mesh, in_specs=placed, out_specs=P("row", "col"), check_vma=False
    )
```

profile of v0, /device:TPU:19, one launch (start us, length us, event | category | flops | bytes accessed | tf_op | source)
XLA Modules:
  0.0 607.3 jit_solution(13421771555223509871)
XLA Ops:
  6.5 0.7 all-gather.5.cloned.1.call-update
  7.3 0.7 all-gather.3.cloned.1.call-update
  8.0 28.9 %all-gather.5.cloned.1.call-done = bf16[32,16384]{1,0:T(8,128)(2,1)} async-done(((bf16[32,2048]{1,0:T(8,128)(2,1)}), bf16[32,16384]{1,0:T(8,128)(2,1)}) %all-gather.5.cloned.1.call-update) | async-done | bytes 1048592 | tf_op jit(solution)/shard_map/all_gather | solution.py:47
  36.9 1.8 reshape.103
  38.8 1.5 copy.43
  40.3 9.6 %all-to-all-start = ((bf16[32,32,512]{2,0,1:T(8,128)(2,1)}), bf16[32,32,512]{2,0,1:T(8,128)(2,1)S(1)}, u32[]{:S(2)}, u32[]{:S(2)}) async-start(bf16[32,32,512]{2,0,1:T(8,128)(2,1)} %bitcast.2), calls=%async_computation | async-start | bytes 2097152 | tf_op jit(solution)/shard_map/all_to_all | solution.py:57
  50.0 27.5 %all-to-all-done = bf16[32,32,512]{2,0,1:T(8,128)(2,1)S(1)} async-done(((bf16[32,32,512]{2,0,1:T(8,128)(2,1)}), bf16[32,32,512]{2,0,1:T(8,128)(2,1)S(1)}, u32[]{:S(2)}, u32[]{:S(2)}) %all-to-all-start) | async-done | bytes 1048608 | tf_op jit(solution)/shard_map/all_to_all | solution.py:57
  77.5 45.0 %all-gather.3.cloned.1.call-done = bf16[1024,2048]{1,0:T(8,128)(2,1)} async-done(((bf16[32,2048]{1,0:T(8,128)(2,1)}), bf16[1024,2048]{1,0:T(8,128)(2,1)}) %all-gather.3.cloned.1.call-update) | async-done | bytes 4194320 | tf_op jit(solution)/shard_map/all_gather | solution.py:60
  122.6 6.2 %select_add_fusion = f32[2048,512]{1,0:T(8,128)S(1)} fusion(f32[2048,512]{1,0:T(8,128)} %param.4, bf16[1024,2048]{1,0:T(8,128)(2,1)} %all-gather.3.cloned.1.call-done, bf16[1024,512]{1,0:T(8,128)(2,1)S(1)} %bitcast.76, f32[2048]{0:T(1024)S(1)} %copy-done.5, s32[512]{0:T(512)S(1)} %fusion.58, s32[2048]{0:T(1024)S(1)} %fusion.49), kind=kOutput, calls=%fused_computation.7 | convolution fusion | flops 2152726528 | bytes 13649920 | tf_op jit(solution)/shard_map/dot_general | solution.py:59
  128.8 2.0 copy-done
  130.8 0.9 fusion.22
  131.7 0.2 all-reduce.8.cloned.1.call-start
  132.0 63.7 %all-reduce.6.cloned.1.call-done = bf16[512,512]{1,0:T(8,128)(2,1)} async-done(((bf16[512,512]{1,0:T(8,128)(2,1)}), bf16[512,512]{1,0:T(8,128)(2,1)}) %all-reduce.6.cloned.1.call-update) | async-done | bytes 524304 | tf_op jit(solution)/shard_map/psum | solution.py:11
  195.7 1.2 convert_select_fusion.1
  196.9 0.3 copy.30
  197.2 1.3 fusion.16
  198.5 0.3 copy.31
  198.9 0.2 fusion.19
  199.1 11.7 %cholesky.103 = f32[128,128]{1,0:T(8,128)S(1)} custom-call(f32[128,128]{1,0:T(8,128)S(1)} %cholesky.263), custom_call_target="Cholesky" | custom-call | tf_op jit(solution)/shard_map/jit(cholesky)/cholesky | solution.py:20
  210.9 9.8 %custom-call.31 = f32[1,128,128]{1,2,0:T(8,128)S(1)} custom-call(f32[1,128,128]{2,1,0:T(8,128)S(1)} %get-tuple-element.34), custom_call_target="InvertDiagBlocksLowerTriangular" | custom-call | tf_op jit(solution)/shard_map/jit(cholesky)/cholesky | solution.py:20
  220.7 0.1 cholesky.222
  220.8 0.3 constant_dynamic-update-slice_fusion.3
  221.1 0.3 convolution_subtract_fusion.2
  221.5 11.7 %cholesky.215 = f32[128,128]{1,0:T(8,128)S(1)} custom-call(f32[128,128]{1,0:T(8,128)S(1)} %cholesky.267), custom_call_target="Cholesky" | custom-call | tf_op jit(solution)/shard_map/jit(cholesky)/cholesky | solution.py:20
  233.2 10.2 %custom-call.32 = f32[1,128,128]{1,2,0:T(8,128)S(1)} custom-call(f32[1,128,128]{2,1,0:T(8,128)S(1)} %get-tuple-element.31), custom_call_target="InvertDiagBlocksLowerTriangular" | custom-call | tf_op jit(solution)/shard_map/jit(cholesky)/cholesky | solution.py:20
  243.4 0.3 convolution_dynamic-update-slice_fusion
  243.7 0.4 convolution_subtract_fusion.3
  244.1 11.7 %cholesky.236 = f32[128,128]{1,0:T(8,128)S(1)} custom-call(f32[128,128]{1,0:T(8,128)S(1)} %cholesky.272), custom_call_target="Cholesky" | custom-call | tf_op jit(solution)/shard_map/jit(cholesky)/cholesky | solution.py:20
  255.8 0.6 compare_reduce_fusion.1
  256.4 9.8 %custom-call.33 = f32[1,128,128]{1,2,0:T(8,128)S(1)} custom-call(f32[1,128,128]{2,1,0:T(8,128)S(1)} %get-tuple-element.28), custom_call_target="InvertDiagBlocksLowerTriangular" | custom-call | tf_op jit(solution)/shard_map/jit(cholesky)/cholesky | solution.py:20
  266.3 0.2 convolution_dynamic-update-slice_fusion.1
  266.5 0.4 convolution_subtract_fusion.4
  266.9 11.9 %cholesky.253 = f32[128,128]{1,0:T(8,128)S(1)} custom-call(f32[128,128]{1,0:T(8,128)S(1)} %convolution_subtract_fusion.4), custom_call_target="Cholesky" | custom-call | tf_op jit(solution)/shard_map/jit(cholesky)/cholesky | solution.py:20
  278.8 0.7 compare_reduce_fusion
  279.4 0.7 compare_reduce_fusion.2
  282.5 1.3 fusion.20
  283.8 10.1 %while.1 = (s32[]{:T(128)}, f32[512,512]{1,0:T(8,128)S(1)}, s32[4,2]{0,1:T(2,128)S(1)}, f32[4,128,128]{2,1,0:T(8,128)}, s32[]{:T(128)}) while((s32[]{:T(128)}, f32[512,512]{1,0:T(8,128)S(1)}, s32[4,2]{0,1:T(2,128)S(1)}, f32[4,128,128]{2,1,0:T(8,128)}, s32[]{:T(128)}) %tuple.28), condition=%wide.while_cond, body=%wide.while_body.sunk | while | flops 2 | bytes 132705 | solution.py:24
  283.8 0.1 constant_dynamic-slice_fusion.2
  283.9 0.5 fusion.75
  284.4 1.9 bitcast_dynamic-update-slice_fusion.2
  286.3 0.1 constant_dynamic-slice_fusion.2
  286.4 0.5 fusion.75
  286.9 1.9 bitcast_dynamic-update-slice_fusion.2
  288.8 0.1 constant_dynamic-slice_fusion.2
  288.9 0.5 fusion.75
  289.4 1.9 bitcast_dynamic-update-slice_fusion.2
  291.4 0.5 fusion.75
  291.9 1.9 bitcast_dynamic-update-slice_fusion.2
  293.9 40.2 %custom-call.34 = f32[4,128,128]{1,2,0:T(8,128)S(1)} custom-call(f32[4,128,128]{2,1,0:T(8,128)} %get-tuple-element.12), custom_call_target="InvertDiagBlocksLowerTriangular" | custom-call | tf_op jit(solution)/shard_map/jit(_solve_triangular)/triangular_solve | solution.py:24
  334.0 2.4 fusion.17
  336.5 3.0 convolution_subtract_fusion.1
  339.5 1.1 fusion.34
  340.6 3.5 convolution_subtract_fusion
  344.2 1.1 fusion.32
  345.3 7.3 %fusion.9 = f32[128,2048]{0,1:T(8,128)} fusion(f32[128,2048]{1,0:T(8,128)S(1)} %fusion.32, f32[128,2048]{1,0:T(8,128)S(1)} %fusion.34, f32[128,2048]{1,0:T(8,128)S(1)} %fusion.17, f32[512,2048]{0,1:T(8,128)S(1)} %bitcast.74, f32[512,512]{1,0:T(8,128)} %copy-done.4), kind=kOutput, calls=%fused_computation.14 | convolution fusion | flops 1209794560 | bytes 5439488 | tf_op jit(solution)/shard_map/jit(_solve_triangular)/triangular_solve | solution.py:24
  352.5 1.4 copy.37
  353.9 1.3 copy.36
  355.2 1.3 copy.35
  356.5 1.0 fusion.31
  357.5 3.7 fusion.2
  361.3 162.6 %all-reduce.8.cloned.1.call-done = f32[2048,512]{1,0:T(8,128)} async-done(((f32[2048,512]{1,0:T(8,128)}), f32[2048,512]{1,0:T(8,128)}) %all-reduce.8.cloned.1.call-update) | async-done | bytes 4194320 | tf_op jit(solution)/shard_map/psum | solution.py:11
  523.9 2.2 fusion.21
  526.1 64.0 %all-reduce.10.cloned.1.call-done = bf16[512,512]{1,0:T(8,128)(2,1)} async-done(((bf16[512,512]{1,0:T(8,128)(2,1)}), bf16[512,512]{1,0:T(8,128)(2,1)}) %all-reduce.10.cloned.1.call-update) | async-done | bytes 524304 | tf_op jit(solution)/shard_map/psum | solution.py:11
  590.1 10.4 %fusion = f32[2048,512]{1,0:T(8,128)} fusion(f32[2048,512]{1,0:T(8,128)} %all-reduce.8.cloned.1.call-done, f32[2048,512]{1,0:T(8,128)} %copy-done, bf16[512,512]{1,0:T(8,128)(2,1)} %all-reduce.10.cloned.1.call-done, pred[2048]{0:T(1024)(128)(4,1)S(1)} %broadcast_compare_fusion, pred[512]{0:T(512)(128)(4,1)S(1)} %broadcast_compare_fusion.1), kind=kOutput, calls=%fused_computation.3 | convolution fusion | flops 6445596672 | bytes 13109760 | tf_op jit(solution)/shard_map/dot_general | solution.py:80
  (34 shorter events, 0.5 us)
Async XLA Ops:
  6.5 116.0 %copy-start.5 = (f32[2048]{0:T(1024)S(1)}, f32[2048]{0:T(1024)}, u32[]{:S(2)}) copy-start(f32[2048]{0:T(1024)} %param.5) | copy-start | bytes 24580
  6.5 30.4 %all-gather.5.cloned.1.call-start = ((), (), s32[]{:S(2)}) async-start(), calls=%async_computation.2 | async-start | bytes 1179648 | tf_op jit(solution)/shard_map/all_gather | solution.py:47
  7.3 115.3 %all-gather.3.cloned.1.call-start = ((), (), s32[]{:S(2)}) async-start(), calls=%async_computation.1 | async-start | bytes 4325376 | tf_op jit(solution)/shard_map/all_gather | solution.py:60
  40.3 37.2 %all-to-all-start = ((bf16[32,32,512]{2,0,1:T(8,128)(2,1)}), bf16[32,32,512]{2,0,1:T(8,128)(2,1)S(1)}, u32[]{:S(2)}, u32[]{:S(2)}) async-start(bf16[32,32,512]{2,0,1:T(8,128)(2,1)} %bitcast.2), calls=%async_computation | async-start | bytes 2097152 | tf_op jit(solution)/shard_map/all_to_all | solution.py:57
  49.9 145.8 %all-reduce.6.cloned.1.call-start = ((), (), s32[]{:S(2)}) async-start(), calls=%async_computation.3 | async-start | bytes 1048576 | tf_op jit(solution)/shard_map/psum | solution.py:11
  128.8 2.0 copy-start
  131.7 392.2 %all-reduce.8.cloned.1.call-start = ((), (), s32[]{:S(2)}) async-start(), calls=%async_computation.4 | async-start | bytes 8388608 | tf_op jit(solution)/shard_map/psum | solution.py:11
  293.9 46.8 %copy-start.4 = (f32[512,512]{1,0:T(8,128)}, f32[512,512]{1,0:T(8,128)S(1)}, u32[]{:S(2)}) copy-start(f32[512,512]{1,0:T(8,128)S(1)} %get-tuple-element.91) | copy-start | bytes 3145732
  334.0 6.6 %copy-start.1 = (f32[2048,512]{1,0:T(8,128)S(1)}, f32[2048,512]{1,0:T(8,128)}, u32[]{:S(2)}) copy-start(f32[2048,512]{1,0:T(8,128)} %copy-done) | copy-start | bytes 12582916
  353.9 2.6 copy-start.2
  355.2 2.3 copy-start.3
  361.2 228.8 %all-reduce.10.cloned.1.call-start = ((), (), s32[]{:S(2)}) async-start(), calls=%async_computation.5 | async-start | bytes 1048576 | tf_op jit(solution)/shard_map/psum | solution.py:11
Sparse Core Ops, SparseCore 0:
  9.2 27.6 all-gather.4
  39.5 83.0 all-gather.2
  131.9 63.8 all-reduce.5
  361.4 162.5 all-reduce.7
  526.2 63.8 all-reduce.9
where the time goes:
time: 615 us; the launch traced here: 607 us
  waiting for transfers between devices  393 us (64%)
  other arithmetic  130 us (21%)
  matrix products  37.9 us (6%)
  local copies, waits for them, and re-layouts  20.3 us (3%)
  between operations  16.1 us (3%)
  starting transfers between devices  9.92 us (2%)
    psum x3, waiting for transfers between devices, from_root(): return lax.psum(block, axis)  290 us
    another operation x14, other arithmetic, factor_corner(): return jnp.linalg.cholesky(symmetric)  78.9 us
    all_gather x1, waiting for transfers between devices, on_device(): lax.all_gather(span, 'col', axis=0, tiled=True)  45 us
    another operation x3, other arithmetic, apply_factor(): jax.scipy.linalg.solve_triangular(lower_part, panel_source.T, lower=True)  41.4 us
    all_gather x1, waiting for transfers between devices, on_device(): full = lax.all_gather(span, 'row', axis=1, tiled=True)  28.9 us
    all_to_all x1, waiting for transfers between devices, on_device(): lax.all_to_all(grouped, 'col', split_axis=1, concat_axis=0, tiled=True)  27.5 us
    another operation x7, matrix products, apply_factor(): jax.scipy.linalg.solve_triangular(lower_part, panel_source.T, lower=True)  19.4 us
  transfers between devices with their start and end apart: 6, of which 6 were waited for; matrix products, arithmetic and copies ran while one was open for 1% of the time, Pallas kernels for 0%

commit v1 on v0

v1 whole, which is shorter than its diff:
```python
import jax
import jax.numpy as jnp
from jax import lax
from jax.experimental import pallas as pl
from jax.experimental.pallas import tpu as pltpu
from jax.sharding import PartitionSpec as P

NB = 512
NX, NZ, NROW = 4, 8, 8
NCOL = NX * NZ
TOKENS = 1024
ORDER = (0, -1, 1, -2, 2, -3, 3, 4)
MESH = pl.DeviceIdType.MESH
HI = lax.Precision.HIGHEST
F32, BF16 = jnp.float32, jnp.bfloat16
TN = (((0,), (0,)), ((), ()))


def eye(n):
    return (lax.broadcasted_iota(jnp.int32, (n, n), 0)
            == lax.broadcasted_iota(jnp.int32, (n, n), 1)).astype(F32)


def factor_block(d, between):
    n = d.shape[0]
    rows = lax.broadcasted_iota(jnp.int32, (8, n), 0)
    e = eye(n)
    done = []
    for p in range(n // 8):
        left = n - 8 * p
        if p % 4 == 0:
            between(p // 4)
        cols = [jnp.broadcast_to(d[:, 8 * p + j:8 * p + j + 1], (left, n)) for j in range(8)]
        pivots = jnp.ones((8, n), F32)
        for j in range(8):
            pivot = cols[j][j:j + 1]
            pivots = jnp.where(rows == j, pivot, pivots)
            f = cols[j] * (1.0 / pivot)
            head = jnp.where(rows > j, f[:8], 0.0)
            f = jnp.concatenate([head, f[8:]], axis=0) if left > 8 else head
            d = d - f * d[j:j + 1]
            e = e - f * e[j:j + 1]
            for k in range(j + 1, 8):
                cols[k] = cols[k] - f * cols[k][j:j + 1]
        done.append(e[:8] * lax.rsqrt(pivots))
        if left > 8:
            d, e = d[8:], e[8:]
    return jnp.concatenate(done, axis=0)


def split(a):
    high = a.astype(BF16)
    return high, (a - high.astype(F32)).astype(BF16)


def panel_kernel(span, gram, ridge, acc_out, a0_out, z_out,
                 sg, g0, ea, sc, gc, yg, rr, piece, gv, gb, w, p0, acc, a0, zv,
                 q, ssem, rsem, lsem, pcs, pcr):
    r = lax.axis_index("row")
    c = lax.axis_index("col")
    x, z = c // NZ, c % NZ
    core = r % 2
    other = r + 1 - 2 * core
    zp, zm = x * NZ + (z + 1) % NZ, x * NZ + (z + NZ - 1) % NZ
    xp, xm = (x + 1) % NX * NZ + z, (x + NX - 1) % NX * NZ + z
    xs = {d: (x + NX + d) % NX for d in (-1, 0, 1, 2)}
    zs = {d: (z + NZ + d) % NZ for d in range(-4, 5)}
    receiver = core == z % 2

    number, local_number = {}, {}
    phase = ["go"]

    def index(name):
        return number.setdefault(name, len(number))

    def remote(send_name, name, src, dst, dev):
        return pltpu.make_async_remote_copy(
            src_ref=src, dst_ref=dst, send_sem=ssem.at[index(send_name)], recv_sem=rsem.at[index(name)],
            device_id=dev, device_id_type=MESH)

    def local(name, src, dst):
        i = local_number.setdefault(name, len(local_number))
        return pltpu.make_async_copy(src, dst, lsem.at[i])

    def send(name, src, dst, dev):
        cp = remote(name, name, src, dst, dev)
        if phase[0] == "go":
            cp.start()
        else:
            cp.wait_send()

    def arrive(name, dst):
        if phase[0] == "go":
            remote(name, name, dst, dst, (r, zp)).wait_recv()

    barrier = pltpu.get_barrier_semaphore()
    for d in range(1, NROW):
        pl.semaphore_signal(barrier, inc=1, device_id=((r + d) % NROW, c), device_id_type=MESH)

    @pl.loop(1, NCOL)
    def _(t):
        pl.semaphore_signal(barrier, inc=1, device_id=(r, (c + t) % NCOL), device_id_type=MESH)

    lead, rest = pl.ds(0, NB), pl.ds(NB, 3 * NB)
    lead_in = local("lead", gram.at[lead], gv.at[lead])
    gram_in = local("gram", gram.at[rest], gv.at[rest])
    lead_in.start()
    gram_in.start()
    own = local("own", span, sg.at[x, z])
    own.start()

    def cast_panel(lo, hi):
        @pl.loop(lo, hi)
        def _(t):
            part = pl.ds(pl.multiple_of(t * 256, 256), 256)
            gb[part, :] = gv[part, :].astype(BF16)

    @pl.when(c == 0)
    def _():
        lead_in.wait()
        cast_panel(0, 2)
        gram_in.wait()
        cast_panel(2, 8)

    pl.semaphore_wait(barrier, NROW - 1 + NCOL - 1)

    tile0 = pl.ds(0, NB)

    def corner_piece(t):
        return pltpu.make_async_remote_copy(
            src_ref=gb.at[pl.ds(pl.multiple_of(t * 16, 16), 16)], dst_ref=piece,
            send_sem=pcs.at[t], recv_sem=pcr.at[0], device_id=(r, t), device_id_type=MESH)

    @pl.when(jnp.logical_and(r == 0, c == 0))
    def _():
        @pl.loop(1, NCOL)
        def _(t):
            corner_piece(t).start()

    def row0_copies(kind):
        cps = []
        for d in range(1, NROW):
            half = d % 2
            if kind == "g":
                cps.append(remote("g%d" % d, "eg", piece.at[:, pl.ds(half * 256, 256)],
                                  ea.at[x, z, half, :, pl.ds(NB, 256)], (d, c)))
            else:
                cps.append(remote("s%d" % d, "es", span.at[pl.ds(half * 16, 16), tile0],
                                  ea.at[x, z, half, :, pl.ds(0, NB)], (d, c)))
                cps.append(remote("r%d" % d, "er", ridge.at[pl.ds(0, 8)], rr, (d, c)))
        return cps

    own_s = local("own_s", span.at[pl.ds(0, 16), tile0], ea.at[x, z, 0, :, pl.ds(0, NB)])
    own_g = local("own_g", piece.at[:, pl.ds(0, 256)], ea.at[x, z, 0, :, pl.ds(NB, 256)])
    own_r = local("own_r", ridge.at[pl.ds(0, 8)], rr)

    @pl.when(r == 0)
    def _():
        for cp in row0_copies("s"):
            cp.start()
        own_s.start()
        own_r.start()

    def own_sends():
        send("zp0", span, sg.at[x, z], (r, zp))
        send("zm0", span, sg.at[x, z], (r, zm))
        send("xp0", span, sg.at[x, z], (r, xp))
        send("xm0", span, sg.at[x, z], (r, xm))

    g0_own = local("g0_own", gb.at[pl.ds(0, 64)], g0.at[0, 0])

    hubs = ((NZ, NZ), (3 * NZ, 3 * NZ), (1, 2 * NZ + 1), (NZ - 1, 2 * NZ + 5))

    def hub_copies():
        cps = []
        for hub, first in hubs:
            for h in range(2 if hub % NZ == 0 else 1):
                cps.append(remote("q%d%d" % (hub, h), "q%d" % h, gb.at[pl.ds((first + 4 * h) * 64, 256)],
                                  q.at[pl.ds(4 * h * 64, 256)], (r, hub)))
        cps[-1] = remote("q%d0" % (NZ - 1), "q0", gb.at[pl.ds((2 * NZ + 5) * 64, 192)],
                         q.at[pl.ds(0, 192)], (r, NZ - 1))
        cps.append(remote("q%d1" % (NZ - 1), "q1", gb.at[pl.ds(2 * NZ * 64, 64)],
                          q.at[pl.ds(192, 64)], (r, NZ - 1)))
        for t in range(1, NZ):
            cps.append(remote("p%d" % t, "piece", gb.at[pl.ds(t * 64, 64)], g0.at[0, t], (r, t)))
        return cps

    def hub_pass(h):
        for hub, first in hubs:
            if hub == 1:
                if h:
                    continue
                moves = [(i, 2, 1 + i) for i in range(4)]
            elif hub == NZ - 1:
                moves = [(i, 2, 5 + i) for i in range(3)] if h == 0 else [(3, 2, 0)]
            else:
                moves = [(i, hub // NZ, i) for i in range(4 * h, 4 * h + 4)]

            @pl.when(c == hub)
            def _():
                arrive("q%d" % h, q.at[pl.ds(moves[0][0] * 64, 64 * len(moves))])
                for i, xx, zz in moves:
                    src, dst = q.at[pl.ds(i * 64, 64)], g0.at[xx, zz]
                    if xx * NZ + zz == hub:
                        if phase[0] == "go":
                            local("g0_hub", src, dst).start()
                        continue
                    cp = remote("f%d" % i, "piece", src, dst, (r, xx * NZ + zz))
                    if phase[0] == "go":
                        cp.start()
                    else:
                        cp.wait_send()

    own_sends()

    @pl.when(c == 0)
    def _():
        g0_own.start()
        for cp in hub_copies():
            cp.start()

    def s_arrive():
        @pl.when(r == 0)
        def _():
            own_s.wait()

        @pl.when(r != 0)
        def _():
            arrive("es", ea.at[x, z, core, :, pl.ds(0, NB)])

    def corner_relay():
        @pl.when(r == 0)
        def _():
            @pl.when(c == 0)
            def _():
                cp = local("corner_own", gb.at[pl.ds(0, 16)], piece)
                cp.start()
                cp.wait()

            @pl.when(c != 0)
            def _():
                corner_piece(0).wait_recv()

            for cp in row0_copies("g"):
                cp.start()
            own_g.start()

    def corner_arrive():
        @pl.when(r == 0)
        def _():
            own_g.wait()
            own_r.wait()

        @pl.when(r != 0)
        def _():
            arrive("eg", ea.at[x, z, core, :, pl.ds(NB, 256)])
            arrive("er", rr)

    def block(xx, zz):
        return sg.at[xx, zz]

    def block_lo(xx, zz):
        return sg.at[xx, zz, pl.ds(0, 16)]

    def block_hi(xx, zz):
        return sg.at[xx, zz, pl.ds(16, 16)]

    def span_z(s):
        full = s < 4
        arrive("zp%d" % (s - 1), (block if full else block_lo)(x, zs[-s]))
        arrive("zm%d" % (s - 1), (block if full else block_hi)(x, zs[s]))
        if s < 4:
            p, m = (block, block) if s < 3 else (block_lo, block_hi)
            send("zp%d" % s, p(x, zs[-s]), p(x, zs[-s]), (r, zp))
            send("zm%d" % s, m(x, zs[s]), m(x, zs[s]), (r, zm))

    def span_x(k):
        b = block(x, zs[ORDER[k]])
        send("xp%d" % k, b, b, (r, xp))
        send("xm%d" % k, b, b, (r, xm))

    def span_relay(k):
        zz = zs[ORDER[k]]
        arrive("xp%d" % k, block(xs[-1], zz))
        send("xxp%d" % k, block_lo(xs[-1], zz), block_lo(xs[-1], zz), (r, xp))
        arrive("xm%d" % k, block(xs[1], zz))
        send("xxm%d" % k, block_hi(xs[1], zz), block_hi(xs[1], zz), (r, xm))

    def span_end(k):
        zz = zs[ORDER[k]]
        arrive("xxp%d" % k, block_lo(xs[2], zz))
        arrive("xxm%d" % k, block_hi(xs[2], zz))

    x2 = (x + 2) % NX * NZ + z

    lanes_of = {"s": pl.ds(0, NB), "g": pl.ds(NB, 256)}

    def e_z_send(kind):
        b = ea.at[x, z, core, :, lanes_of[kind]]
        for d in range(1, NZ):
            send("ez%s%d" % (kind, d), b, b, (r, x * NZ + (z + d) % NZ))

    def e_z_arrive(kind):
        for d in range(1, NZ):
            arrive("ez%s%d" % (kind, d), ea.at[x, (z + NZ - d) % NZ, core, :, lanes_of[kind]])

    def e_core(kind, d):
        b = ea.at[xs[d], :, core, :, lanes_of[kind]]
        send("ec%s%d" % (kind, d), b, b, (other, c))

    def e_x_send(kind):
        b = ea.at[x, :, core, :, lanes_of[kind]]
        send("exp" + kind, b, b, (r, xp))
        send("exm" + kind, b, b, (r, xm))
        send("ex2" + kind, b, b, (r, x2))
        e_core(kind, 0)

    def e_x_arrive(kind):
        for tag, d in (("exp", -1), ("exm", 1), ("ex2", 2)):
            arrive(tag + kind, ea.at[xs[d], :, core, :, lanes_of[kind]])
            e_core(kind, d)

    def e_core_arrive():
        for kind in "sg":
            for d in (0, -1, 1, 2):
                arrive("ec%s%d" % (kind, d), ea.at[xs[d], :, 1 - core, :, lanes_of[kind]])

    def g_arrive():
        if phase[0] != "go":
            return

        direct = jnp.logical_and(jnp.logical_and(c != 0, c != NZ), c != 3 * NZ)

        @pl.when(direct)
        def _():
            arrive("piece", g0.at[x, z])

        @pl.when(jnp.logical_or(c == NZ, c == 3 * NZ))
        def _():
            local("g0_hub", q.at[pl.ds(0, 64)], g0.at[x, z]).wait()

        @pl.when(c == 0)
        def _():
            g0_own.wait()

    def g_x_send():
        b = g0.at[x, z]
        send("gxp", b, b, (r, xp))
        send("gxm", b, b, (r, xm))
        send("gx2", b, b, (r, x2))
        for d in (1, 2, 3):
            send("yg%d" % d, b, yg.at[d - 1], ((r + 2 * d) % NROW, c))

    def g_x_arrive(j):
        arrive(("gxp", "gxm", "gx2")[j - 1], g0.at[xs[(0, -1, 1, 2)[j]], z])

    def g_z(j, s):
        xx = xs[(0, -1, 1, 2)[j]]
        for sign, tag, peer in ((-1, "p", zp), (1, "m", zm)):
            b = g0.at[xx, zs[sign * s]]
            if s >= 3:
                half = g0.at[xx, zs[sign * s], pl.ds(0 if tag == "p" else 32, 32)]
            if s:
                arrive("gz%s%d%d" % (tag, j, s - 1), half if s == 4 else b)
            if s < 4:
                h = half if s == 3 else b
                send("gz%s%d%d" % (tag, j, s), h, h, (r, peer))

    def route(name, src, dst, target):
        if phase[0] != "near":
            @pl.when(target != c)
            def _():
                far = remote(name, name.rstrip("0123456789"), src, dst, (r, target))
                if phase[0] == "go":
                    far.start()
                else:
                    far.wait_send()

        if phase[0] != "drain":
            @pl.when(target == c)
            def _():
                near = local(name, src, dst)
                if phase[0] == "go":
                    near.start()
                else:
                    near.wait()

    is_source = r == z
    relays = jnp.logical_and(receiver, jnp.logical_not(is_source))
    tile = pl.ds(pl.multiple_of(x * NB, NB), NB)

    def share(k):
        zz = zs[ORDER[k]]
        src, dst = sg.at[:, zz, :, tile], sc.at[:, zz]

        @pl.when(is_source)
        def _():
            for tag, dev in (("c", other), ("2", (r + 2) % NROW), ("6", (r + 6) % NROW), ("4", (r + 4) % NROW)):
                cp = remote("sh%d_%s" % (k, tag), "sh%d" % k, src, dst, (dev, c))
                if phase[0] == "go":
                    cp.start()
                else:
                    cp.wait_send()
            if phase[0] == "go":
                local("sh%d" % k, src, dst).start()

    def share_next(k):
        zz = zs[ORDER[k]]
        src, dst = sg.at[:, zz, :, tile], sc.at[:, zz]
        if phase[0] == "go":
            @pl.when(is_source)
            def _():
                local("sh%d" % k, src, dst).wait()

            @pl.when(jnp.logical_not(is_source))
            def _():
                arrive("sh%d" % k, dst)

        @pl.when(relays)
        def _():
            cp = remote("sh%d_c" % k, "sh%d" % k, dst, dst, (other, c))
            if phase[0] == "go":
                cp.start()
            else:
                cp.wait_send()

    def gc_routes():
        for d in range(4):
            row = (r + NROW - 2 * d) % NROW
            if d:
                arrive("yg%d" % d, yg.at[d - 1])
            route("gc%d" % d, yg.at[d - 1] if d else g0.at[x, z], gc.at[z], x * NZ + row)

    def forward(name, ref, part, piece_name, routes):
        if phase[0] == "go":
            phase[0] = "near"
            routes()
            phase[0] = "go"

        @pl.when(receiver)
        def _():
            arrive(piece_name, part)
            send(name, ref, ref, (other, c))

    def gc_forward():
        forward("gcf", gc, gc.at[pl.ds(0, NZ - 1)], "gc", gc_routes)

    def shared_arrive():
        @pl.when(jnp.logical_not(receiver))
        def _():
            arrive("gcf", gc)

    span_z(1)
    span_x(1)
    span_x(2)
    s_arrive()
    e_z_send("s")
    hub_pass(0)
    corner_relay()
    span_z(2)
    hub_pass(1)
    span_relay(0)
    corner_arrive()
    e_z_send("g")
    e_z_arrive("s")
    e_x_send("s")
    e_z_arrive("g")
    e_x_send("g")
    span_z(3)
    span_x(3)
    span_x(4)
    span_relay(1)
    g_arrive()
    g_x_send()
    g_z(0, 0)
    e_x_arrive("s")
    e_x_arrive("g")
    span_z(4)
    span_x(5)
    span_x(6)
    span_relay(2)
    for j in (1, 2, 3):
        g_x_arrive(j)
        g_z(j, 0)
    g_z(0, 1)
    span_x(7)
    own.wait()
    e_core_arrive()

    s0 = ea[:, :, :, :, :NB].reshape(TOKENS, NB)
    g00 = jnp.concatenate(
        [ea[:, :, h, :, NB:].reshape(NB, 256) for h in range(2)], axis=1).astype(F32)
    ridge0 = jnp.concatenate([rr[i:i + 1] for i in range(4)], axis=1)
    corner = g00 + lax.dot_general(s0, s0, TN, preferred_element_type=F32) * (1.0 / TOKENS) + eye(NB) * ridge0
    above = lax.broadcasted_iota(jnp.int32, (NB, NB), 0) < lax.broadcasted_iota(jnp.int32, (NB, NB), 1)
    w[:, :NB] = jnp.where(above, corner.T, corner)
    w[:, NB:] = eye(NB)

    slots = [
        lambda: (span_relay(3), span_end(0), share(0)),
        lambda: (g_z(1, 1), g_z(2, 1), g_z(3, 1)),
        lambda: (span_end(1), share(1)),
        lambda: (span_relay(4), gc_routes()),
        lambda: (g_z(0, 2), g_z(1, 2), share_next(0)),
        lambda: (g_z(2, 2), g_z(3, 2)),
        lambda: (span_end(2), share(2), span_relay(5), share_next(1)),
        lambda: (g_z(0, 3), g_z(1, 3)),
        lambda: (span_end(3), share(3), g_z(2, 3), g_z(3, 3)),
        lambda: (span_relay(6), share_next(2)),
        lambda: (span_end(4), share(4), share_next(3)),
        lambda: (span_relay(7), gc_forward()),
        lambda: (span_end(5), share(5), share_next(4)),
        lambda: [g_z(j, 4) for j in range(4)],
        lambda: (span_end(6), share(6), share_next(5)),
        lambda: (span_end(7), share(7), share_next(6)),
    ]
    for kb in range(NB // 128):
        lo, hi = kb * 128, kb * 128 + 128
        m = factor_block(w[lo:hi, lo:hi], lambda i: slots[4 * kb + i]())
        head = jnp.dot(m, w[lo:hi, lo:NB + hi], precision=HI, preferred_element_type=F32)
        w[lo:hi, lo:NB + hi] = head
        if hi < NB:
            w[hi:NB, hi:NB + hi] -= lax.dot_general(
                head[:, 128:NB - lo], head[:, 128:], TN, precision=HI, preferred_element_type=F32)

    @pl.when(c != 0)
    def _():
        lead_in.wait()
        gram_in.wait()

    def products(h):
        group = [zs[ORDER[i]] for i in range(4 * h, 4 * h + 4)]
        right = jnp.concatenate([
            jnp.concatenate([sc[:, zz].reshape(128, NB), ea[:, zz, :, :, :NB].reshape(128, NB)], axis=1)
            for zz in group], axis=0)

        @pl.loop(0, NROW // 2)
        def _(k):
            part = pl.ds(pl.multiple_of(k * NB, NB), NB)
            a = jnp.concatenate([sg[:, zz, :, part].reshape(128, NB) for zz in group], axis=0)
            prod = lax.dot_general(a, right, TN, preferred_element_type=F32) * (1.0 / TOKENS)
            if h:
                acc[part, :] += prod[:, :NB]
                a0[part, :] = (p0[part, :] + prod[:, NB:] + g0[k].reshape(NB, NB).astype(F32)).astype(BF16)
            else:
                acc[part, :] = prod[:, :NB] + gv[part, :]
                p0[part, :] = prod[:, NB:]

                @pl.when(jnp.logical_and(r == z, k == x))
                def _():
                    four = ridge[pl.ds(4 * k, 4), :]
                    acc[part, :] += eye(NB) * jnp.concatenate([four[i:i + 1] for i in range(4)], axis=1)

    products(0)
    shared_arrive()
    share_next(7)

    @pl.when(c != 0)
    def _():
        ac0 = gc[...].reshape(NB, NB).astype(F32) + lax.dot_general(
            sc[...].reshape(TOKENS, NB), ea[:, :, :, :, :NB].reshape(TOKENS, NB), TN, preferred_element_type=F32) * (1.0 / TOKENS)
        high, low = split(w[:, NB:])
        b = ac0.astype(BF16)
        nt = (((1,), (1,)), ((), ()))
        y = (lax.dot_general(high, b, nt, preferred_element_type=F32)
             + lax.dot_general(low, b, nt, preferred_element_type=F32)).astype(BF16)
        zv[...] = (lax.dot_general(high, y, TN, preferred_element_type=F32)
                   + lax.dot_general(low, y, TN, preferred_element_type=F32)).astype(BF16)

    @pl.when(c == 0)
    def _():
        zv[...] = (-w[:, NB:].T).astype(BF16)

    z_copy = local("z_out", zv, z_out)
    z_copy.start()
    products(1)

    @pl.when(r == 0)
    def _():
        a0[:NB, :] = jnp.zeros((NB, NB), BF16)

    @pl.when(c == 0)
    def _():
        acc[...] = jnp.zeros(acc.shape, F32)

        @pl.when(r == 0)
        def _():
            acc[:NB, :] = jnp.where(above, 0.0, w[:, :NB].T)

    a_copies = [local("a0_out", a0, a0_out), local("acc_out", acc, acc_out)]
    for cp in a_copies:
        cp.start()

    phase[0] = "drain"
    own_sends()
    hub_pass(0)
    hub_pass(1)
    for kind in "sg":
        e_z_send(kind)
        e_x_send(kind)
        e_x_arrive(kind)
    g_x_send()
    for s in range(5):
        for j in range(4):
            g_z(j, s)
    for s in range(1, 5):
        span_z(s)
    for k in range(8):
        if k:
            span_x(k)
        span_relay(k)
    for k in range(8):
        share(k)
        share_next(k)
    gc_routes()
    gc_forward()

    @pl.when(r == 0)
    def _():
        for cp in row0_copies("s") + row0_copies("g"):
            cp.wait_send()

    @pl.when(c == 0)
    def _():
        for cp in hub_copies():
            cp.wait_send()

        @pl.when(r == 0)
        def _():
            @pl.loop(1, NCOL)
            def _(t):
                corner_piece(t).wait_send()

    for cp in [z_copy] + a_copies:
        cp.wait()


def panel(span, gram, ridge):
    rows, cols = gram.shape
    dma = pltpu.SemaphoreType.DMA
    scratch = [
        ((NX, NZ, 32, rows), BF16), ((NX, NZ, 64, NB), BF16), ((NX, NZ, 2, 16, 768), BF16),
        ((NX, NZ, 32, NB), BF16), ((NZ, 64, NB), BF16), ((3, 64, NB), BF16),
        ((8, 128), F32), ((16, NB), BF16), ((rows, cols), F32), ((rows, cols), BF16),
        ((NB, 2 * NB), F32), ((rows, cols), F32), ((rows, cols), F32), ((rows, cols), BF16),
        ((NB, NB), BF16)]
    return pl.pallas_call(
        panel_kernel,
        out_shape=[jax.ShapeDtypeStruct((rows, cols), F32), jax.ShapeDtypeStruct((rows, cols), BF16),
                   jax.ShapeDtypeStruct((NB, NB), BF16)],
        in_specs=[pl.BlockSpec(memory_space=pl.ANY)] * 2 + [pl.BlockSpec(memory_space=pltpu.VMEM)],
        out_specs=[pl.BlockSpec(memory_space=pl.ANY)] * 3,
        scratch_shapes=[pltpu.VMEM(*s) for s in scratch] + [
            pltpu.VMEM((NB, NB), BF16), dma((240,)), dma((240,)), dma((40,)), dma((NCOL,)), dma((1,))],
        compiler_params=pltpu.CompilerParams(
            collective_id=0, has_side_effects=True, vmem_limit_bytes=56 * 2**20),
    )(span, gram, ridge.reshape(16, 128))


def finish_kernel(acc, a0, zc, out):
    out[...] = acc[...] - jnp.dot(a0[...], zc[...], preferred_element_type=F32)


def finish(acc, a0, zc):
    rows, cols = acc.shape
    step = 1024
    return pl.pallas_call(
        finish_kernel,
        grid=(rows // step,),
        out_shape=jax.ShapeDtypeStruct((rows, cols), F32),
        in_specs=[pl.BlockSpec((step, cols), lambda i: (i, 0)), pl.BlockSpec((step, NB), lambda i: (i, 0)),
                  pl.BlockSpec((NB, cols), lambda i: (0, 0))],
        out_specs=pl.BlockSpec((step, cols), lambda i: (i, 0)),
    )(acc, a0, zc)


def on_device(span, gram, ridge):
    return finish(*panel(span, gram, ridge))


def solution(mesh):
    placed = (P("col", "row"), P("row", "col"), P("row"))
    return jax.shard_map(
        on_device, mesh=mesh, in_specs=placed, out_specs=P("row", "col"), check_vma=False
    )
```

time: 615 us -> 113 us (0.18); the launches traced: 607 us -> 113 us
  waiting for transfers between devices: 393 us -> 0 us
  other arithmetic: 130 us -> 0 us
  Pallas kernels: 0 us -> 113 us
  matrix products: 37.9 us -> 0 us
  local copies, waits for them, and re-layouts: 20.3 us -> 0 us
  between operations: 16.1 us -> 0.01 us
  starting transfers between devices: 9.92 us -> 0 us
    psum x3 -> x0, waiting for transfers between devices: 290 us -> none  [from_root(): return lax.psum(block, axis)]
    another operation x17 -> x0, other arithmetic: 120 us -> none  [the longest x14 78.9 us: factor_corner(): return jnp.linalg.cholesky(symmetric)]
    pallas_call x0 -> x2, Pallas kernels: none -> 113 us  [the longest x1 108 us: panel(): pl.pallas_call(panel_kernel, out_shape=[jax.ShapeDtypeStruct((rows, cols)...]
    all_gather x2 -> x0, waiting for transfers between devices: 73.9 us -> none  [the longest x1 45 us: on_device(): lax.all_gather(span, 'col', axis=0, tiled=True)]
    all_to_all x1 -> x0, waiting for transfers between devices: 27.5 us -> none  [on_device(): lax.all_to_all(grouped, 'col', split_axis=1, concat_axis=0, tiled=True)]
    another operation x13 -> x0, matrix products: 21.3 us -> none  [the longest x7 19.4 us: apply_factor(): jax.scipy.linalg.solve_triangular(lower_part, panel_source.T, lower=True)]
    dot_general x2 -> x0, matrix products: 16.6 us -> none  [the longest x1 10.4 us: on_device(): lax.dot_general(panel, matched_parts, (((1,), (1,)), ((), ())), precision...]
    another operation x21 -> x0, local copies, waits for them, and re-layouts: 15.8 us -> none
  transfers between devices with their start and end apart: 6 -> 0, of which waited for: 6 -> 0; matrix products, arithmetic and copies ran while one was open for 1% -> 0% of each run, Pallas kernels for 0% -> 0%
where the time goes in v1:
time: 113 us
  Pallas kernels  113 us (100%)
    pallas_call x1, Pallas kernels, panel(): pl.pallas_call(panel_kernel, out_shape=[jax.ShapeDtypeStruct((rows, cols)...  108 us
    pallas_call x1, Pallas kernels, finish(): pl.pallas_call(finish_kernel, grid=(rows // step,), out_shape=jax.ShapeDt...  4.99 us

profile of v1, /device:TPU:19, one launch (start us, length us, event | category | flops | bytes accessed | tf_op | source)
XLA Modules:
  0.0 112.9 jit_solution(1314486493297640088)
XLA Ops:
  0.0 107.9 %shard_map.37 = (f32[2048,512]{1,0:T(8,128)}, bf16[2048,512]{1,0:T(8,128)(2,1)}, bf16[512,512]{1,0:T(8,128)(2,1)}) custom-call(bf16[32,2048]{1,0:T(8,128)(2,1)} %span.1, f32[2048,512]{1,0:T(8,128)} %gram.1, f32[16,128]{1,0:T(8,128)} %bitcast.1), custom_call_target="tpu_custom_call" | custom-call | tf_op jit(solution)/shard_map/pallas_call | solution.py:647
  107.9 5.0 %shard_map.38 = f32[2048,512]{1,0:T(8,128)} custom-call(f32[2048,512]{1,0:T(8,128)} %get-tuple-element.8.acc, bf16[2048,512]{1,0:T(8,128)(2,1)} %get-tuple-element.9.a0, bf16[512,512]{1,0:T(8,128)(2,1)} %get-tuple-element.10.zc), custom_call_target="tpu_custom_call" | custom-call | tf_op jit(solution)/shard_map/pallas_call | solution.py:667
